TPU v7x, 512 devices: a whole 4x4x16 slice. The times are simulated.
512 devices in a mesh: grp: 16 (over x, y), dev: 32 (over z, core).
Axes of the slice: x: 4, y: 4, z: 16, core: 2. Of those that a mesh axis runs over, the one named last changes fastest.
Arguments:
- block_vectors: float32 [262144, 64], P(('grp', 'dev')), may hold values from -6 to 6
- hamiltonian: float32 [4096, 64, 2048], P(('grp', 'dev')), may hold values from -0.125 to 0.125
- pattern: int32 [4096, 32], P(('grp', 'dev')), may hold values from 0 to 4095, as said below
- owned_blocks: int32 [512], P(('grp', 'dev')), may hold values from 1 to 8, as said below
- spectrum: float32 [2], replicated, may hold values from 0.5 to 2
Outputs:
- basis: float32 [262144, 64], P(('grp', 'dev'))
- r_factor: float32 [64, 64], replicated
Inputs may be any that keep to these rules, and one draw needn't show every extreme that they name: pattern[b, 0] = b; every other entry is b + o clipped to the slots, for a distinct nonzero o with |o| <= 16. `owned_blocks`: some device owns all 8 slots.
All inputs are finite; a program needn't handle non-finite values.
Results may differ from a plain program's by a relative error of at most 0.0003.
Values sent between devices are 32-bit elements; how exact they have to be, the bound alone decides.
A program may use at most 64 MiB of HBM per device.

v0:
```python
import jax
import jax.numpy as jnp
from jax import lax
from jax.sharding import PartitionSpec as P

BAND = 16


def shifted(block, axis, distance):
    devices = range(lax.axis_size(axis))
    route = [(i - distance, i) for i in devices if i - distance in devices]
    return lax.ppermute(block, axis, route)


def send_direct(values, distance):
    return shifted(values, ("grp", "dev"), distance)


def extend_band(values, reach_dev):
    lowers = []
    uppers = []
    for distance in range(reach_dev, 0, -1):
        lowers.append(send_direct(values, distance))
    for distance in range(1, reach_dev + 1):
        uppers.append(send_direct(values, -distance))
    return jnp.concatenate(lowers + [values] + uppers, axis=0)


def apply_matrix(values, hamiltonian, local_index, reach_dev):
    extended = extend_band(values, reach_dev)
    block_count, neighbours = local_index.shape
    picked = jnp.take(extended, local_index, axis=0)
    picked = picked.reshape(block_count, neighbours * values.shape[1], values.shape[2])
    return jnp.einsum("gik,gkc->gic", hamiltonian, picked, precision=lax.Precision.HIGHEST)


def summed_gram(flat):
    local_gram = jnp.dot(
        flat.T, flat, precision=lax.Precision.HIGHEST, preferred_element_type=jnp.float32
    )
    return lax.psum(local_gram, ("grp", "dev"))


def cholesky_step(flat):
    gram_total = summed_gram(flat)
    upper = jnp.linalg.cholesky(gram_total).T
    ortho = jax.scipy.linalg.solve_triangular(upper.T, flat.T, lower=True).T
    return (ortho, upper)


def on_device(block_vectors, hamiltonian, pattern, owned_blocks, spectrum):
    block_count = pattern.shape[0]
    block_size = hamiltonian.shape[1]
    columns = block_vectors.shape[1]
    reach_dev = (BAND + block_count - 1) // block_count
    first_block = lax.axis_index(("grp", "dev")) * block_count
    local_index = pattern - first_block + reach_dev * block_count
    live_mask = (jnp.arange(block_count, dtype=jnp.int32) < owned_blocks[0]).astype(jnp.float32)[
        :, None, None
    ]
    shift_value = spectrum[0]
    scale_value = spectrum[1]
    first_vec = block_vectors.reshape(block_count, block_size, columns) * live_mask
    second_vec = live_mask * (
        (apply_matrix(first_vec, hamiltonian, local_index, reach_dev) - shift_value * first_vec)
        / scale_value
    )
    third_vec = live_mask * (
        2.0
        * (apply_matrix(second_vec, hamiltonian, local_index, reach_dev) - shift_value * second_vec)
        / scale_value
        - first_vec
    )
    flat = third_vec.reshape(block_count * block_size, columns)
    ortho_one, upper_one = cholesky_step(flat)
    ortho_two, upper_two = cholesky_step(ortho_one)
    upper_all = jnp.dot(
        upper_two, upper_one, precision=lax.Precision.HIGHEST, preferred_element_type=jnp.float32
    )
    total = jnp.sqrt(
        jnp.float32(block_count * block_size * lax.axis_size("grp") * lax.axis_size("dev"))
    )
    return (ortho_two * total, upper_all / total)


def solution(mesh):
    placed = (
        P(("grp", "dev"), None),
        P(("grp", "dev"), None, None),
        P(("grp", "dev"), None),
        P(("grp", "dev")),
        P(),
    )
    return jax.shard_map(
        on_device,
        mesh=mesh,
        in_specs=placed,
        out_specs=(P(("grp", "dev"), None), P()),
        check_vma=False,
    )
```

profile of v0, /device:TPU:1, one launch (start us, length us, event | category | flops | bytes accessed | tf_op | source)
XLA Modules:
  0.0 355.4 jit_solution(15956783039810358615)
XLA Ops:
  3.7 8.8 %collective-permute-start.2 = (f32[8,64,64]{1,2,0:T(8,128)S(1)}, f32[8,64,64]{1,2,0:T(8,128)S(1)}, u32[]{:S(2)}, u32[]{:S(2)}) collective-permute-start(f32[8,64,64]{1,2,0:T(8,128)S(1)} %copy_multiply_fusion), channel_id=1, source_target_pairs={{1,0},{2,1},{3,2},{4,3},{5,4},{6,5},{7,6},{8,7},{9,8},{10,9},{11,1... | collective-permute-start | bytes 393224 | tf_op jit(solution)/shard_map/ppermute | solution.py:12
  12.5 4.2 %collective-permute-start.1 = (f32[8,64,64]{1,2,0:T(8,128)S(1)}, f32[8,64,64]{1,2,0:T(8,128)S(1)}, u32[]{:S(2)}, u32[]{:S(2)}) collective-permute-start(f32[8,64,64]{1,2,0:T(8,128)S(1)} %copy_multiply_fusion), channel_id=1, source_target_pairs={{0,1},{1,2},{2,3},{3,4},{4,5},{5,6},{6,7},{7,8},{8,9},{9,10},{10,1... | collective-permute-start | bytes 393224 | tf_op jit(solution)/shard_map/ppermute | solution.py:12
  20.8 4.5 %collective-permute-done = f32[8,64,64]{1,2,0:T(8,128)S(1)} collective-permute-done((f32[8,64,64]{1,2,0:T(8,128)S(1)}, f32[8,64,64]{1,2,0:T(8,128)S(1)}, u32[]{:S(2)}, u32[]{:S(2)}) %collective-permute-start) | collective-permute-done | bytes 131104 | tf_op jit(solution)/shard_map/ppermute | solution.py:12
  25.6 4.4 %gather_fusion = f32[256,64,64]{1,2,0:T(8,128)} fusion(f32[40,64,64]{1,2,0:T(8,128)S(1)} %constant_dynamic-update-slice_fusion, s32[1024]{0:T(1024)S(1)} %pad_clamp_fusion), kind=kCustom, calls=%fused_computation.clone | custom fusion | bytes 8389632 | tf_op jit(solution)/shard_map/jit(_take)/gather | solution.py:32
  29.9 3.8 %broadcast_select_fusion.1 = f32[8,32,64,64]{2,3,1,0:T(8,128)S(1)} fusion(f32[8,32,64,64]{2,3,1,0:T(8,128)} %bitcast.73, pred[8,32]{1,0:T(8,128)(4,1)S(1)} %get-tuple-element.4), kind=kLoop, calls=%fused_computation.3 | loop fusion | flops 1048576 | bytes 8388864 | tf_op jit(solution)/shard_map/jit(_take)/select_n | solution.py:32
  33.8 8.0 %copy.15 = f32[8,32,64,64]{2,1,3,0:T(8,128)} copy(f32[8,32,64,64]{2,3,1,0:T(8,128)S(1)} %broadcast_select_fusion.1) | data formatting | bytes 8388608 | tf_op jit(solution)/shard_map/jit(_take)/select_n | solution.py:32
  41.8 7.8 %reshape.35 = f32[8,2048,64]{1,2,0:T(8,128)} reshape(f32[8,32,64,64]{2,1,3,0:T(8,128)} %copy.15) | data formatting | bytes 8388608 | tf_op jit(solution)/shard_map/reshape | solution.py:33
  49.6 8.7 %fusion.4 = f32[8,64,64]{1,2,0:T(8,128)S(1)} fusion(f32[8,2048,64]{1,2,0:T(8,128)} %reshape.35, f32[8,64,2048]{2,1,0:T(8,128)} %param.11, f32[]{:T(128)} %bitcast.4, f32[]{:T(128)} %bitcast.3, f32[8]{0:T(128)S(1)} %compare_convert_fusion, f32[8,64,64]{1,0,2:T(8,128)S(1)} %reshape.34), kind=kOutput, calls=%fused_computation.10 | convolution fusion | flops 805470208 | bytes 8650792 | tf_op jit(solution)/shard_map/gik,gkc->gic/dot_general | solution.py:34
  58.3 4.1 %collective-permute-start.4 = (f32[8,64,64]{1,2,0:T(8,128)S(1)}, f32[8,64,64]{1,2,0:T(8,128)S(1)}, u32[]{:S(2)}, u32[]{:S(2)}) collective-permute-start(f32[8,64,64]{1,2,0:T(8,128)S(1)} %fusion.4), channel_id=1, source_target_pairs={{0,2},{1,3},{2,4},{3,5},{4,6},{5,7},{6,8},{7,9},{8,10},{9,11},{10,... | collective-permute-start | bytes 393224 | tf_op jit(solution)/shard_map/ppermute | solution.py:12
  62.4 2.7 collective-permute-start.5
  68.5 2.8 collective-permute-done.5
  71.3 6.5 %collective-permute-done.6 = f32[8,64,64]{1,2,0:T(8,128)S(1)} collective-permute-done((f32[8,64,64]{1,2,0:T(8,128)S(1)}, f32[8,64,64]{1,2,0:T(8,128)S(1)}, u32[]{:S(2)}, u32[]{:S(2)}) %collective-permute-start.6) | collective-permute-done | bytes 131104 | tf_op jit(solution)/shard_map/ppermute | solution.py:12
  77.9 4.4 %gather_fusion.1 = f32[256,64,64]{1,2,0:T(8,128)} fusion(f32[40,64,64]{1,2,0:T(8,128)S(1)} %constant_dynamic-update-slice_fusion.5, s32[1024]{0:T(1024)S(1)} %pad_clamp_fusion), kind=kCustom, calls=%fused_computation.1.clone | custom fusion | bytes 8389632 | tf_op jit(solution)/shard_map/jit(_take)/gather | solution.py:32
  82.2 3.8 %broadcast_select_fusion = f32[8,32,64,64]{2,3,1,0:T(8,128)S(1)} fusion(f32[8,32,64,64]{2,3,1,0:T(8,128)} %bitcast.72, pred[8,32]{1,0:T(8,128)(4,1)S(1)} %get-tuple-element.4), kind=kLoop, calls=%fused_computation.2 | loop fusion | flops 1048576 | bytes 8388864 | tf_op jit(solution)/shard_map/jit(_take)/select_n | solution.py:32
  86.1 8.0 %copy.16 = f32[8,32,64,64]{2,1,3,0:T(8,128)} copy(f32[8,32,64,64]{2,3,1,0:T(8,128)S(1)} %broadcast_select_fusion) | data formatting | bytes 8388608 | tf_op jit(solution)/shard_map/jit(_take)/select_n | solution.py:32
  94.1 7.8 %reshape.36 = f32[8,2048,64]{1,2,0:T(8,128)} reshape(f32[8,32,64,64]{2,1,3,0:T(8,128)} %copy.16) | data formatting | bytes 8388608 | tf_op jit(solution)/shard_map/reshape | solution.py:33
  101.9 8.7 %fusion.7 = f32[8,64,64]{1,2,0:T(8,128)S(1)} fusion(f32[8,2048,64]{1,2,0:T(8,128)} %reshape.36, f32[8,64,2048]{2,1,0:T(8,128)} %param.11, f32[8,64,64]{1,2,0:T(8,128)S(1)} %fusion.4, f32[]{:T(128)} %bitcast.4, f32[]{:T(128)} %bitcast.3, f32[8]{0:T(128)S(1)} %compare_convert_fusion, f32[8,64,64]{1,0,2:T(8,128)S(1)} %reshape.34), kind=kOutput, calls=%fused_computation.13 | convolution fusion | flops 805535744 | bytes 8781864 | tf_op jit(solution)/shard_map/gik,gkc->gic/dot_general | solution.py:34
  111.1 116.5 %psum.14 = f32[64,64]{0,1:T(8,128)S(1)} all-reduce(f32[64,64]{0,1:T(8,128)S(1)} %convolution_bitcast_fusion.2), channel_id=1, replica_groups=mesh['grp'=16,'dev'=32] {'grp','dev'}, use_global_device_ids=true, to_apply=%region_0.0 | all-reduce | flops 4096 | bytes 32768 | tf_op jit(solution)/shard_map/psum | solution.py:41
  227.9 5.8 %cholesky.44 = f32[64,64]{1,0:T(8,128)S(1)} custom-call(f32[64,64]{1,0:T(8,128)S(1)} %fusion.14), custom_call_target="Cholesky" | custom-call | tf_op jit(solution)/shard_map/jit(cholesky)/cholesky | solution.py:46
  235.1 4.9 %custom-call.6 = f32[1,64,64]{1,2,0:T(8,128)S(1)} custom-call(f32[1,64,64]{2,1,0:T(8,128)S(1)} %fusion.18), custom_call_target="InvertDiagBlocksLowerTriangular" | custom-call | tf_op jit(solution)/shard_map/jit(_solve_triangular)/triangular_solve | solution.py:47
  240.6 99.3 %psum.15 = f32[64,64]{0,1:T(8,128)S(1)} all-reduce(f32[64,64]{0,1:T(8,128)S(1)} %fusion.30), channel_id=1, replica_groups=mesh['grp'=16,'dev'=32] {'grp','dev'}, use_global_device_ids=true, to_apply=%region_3.7 | all-reduce | flops 4096 | bytes 32768 | tf_op jit(solution)/shard_map/psum | solution.py:41
  340.0 5.8 %cholesky.55 = f32[64,64]{1,0:T(8,128)S(1)} custom-call(f32[64,64]{1,0:T(8,128)S(1)} %fusion.12), custom_call_target="Cholesky" | custom-call | tf_op jit(solution)/shard_map/jit(cholesky)/cholesky | solution.py:46
  346.6 2.2 convolution_multiply_fusion.1
  349.5 4.9 %custom-call.7 = f32[1,64,64]{1,2,0:T(8,128)S(1)} custom-call(f32[1,64,64]{2,1,0:T(8,128)S(1)} %select_bitcast_fusion), custom_call_target="InvertDiagBlocksLowerTriangular" | custom-call | tf_op jit(solution)/shard_map/jit(_solve_triangular)/triangular_solve | solution.py:47
  (42 shorter events, 15.4 us)
Async XLA Ops:
  2.4 23.1 %collective-permute-start.3 = (f32[8,64,64]{1,2,0:T(8,128)S(1)}, f32[8,64,64]{1,2,0:T(8,128)S(1)}, u32[]{:S(2)}, u32[]{:S(2)}) collective-permute-start(f32[8,64,64]{1,2,0:T(8,128)S(1)} %copy_multiply_fusion), channel_id=1, source_target_pairs={{2,0},{3,1},{4,2},{5,3},{6,4},{7,5},{8,6},{9,7},{10,8},{11,9},{12,... | collective-permute-start | bytes 393224 | tf_op jit(solution)/shard_map/ppermute | solution.py:12
  3.7 21.8 %collective-permute-start.2 = (f32[8,64,64]{1,2,0:T(8,128)S(1)}, f32[8,64,64]{1,2,0:T(8,128)S(1)}, u32[]{:S(2)}, u32[]{:S(2)}) collective-permute-start(f32[8,64,64]{1,2,0:T(8,128)S(1)} %copy_multiply_fusion), channel_id=1, source_target_pairs={{1,0},{2,1},{3,2},{4,3},{5,4},{6,5},{7,6},{8,7},{9,8},{10,9},{11,1... | collective-permute-start | bytes 393224 | tf_op jit(solution)/shard_map/ppermute | solution.py:12
  12.5 12.9 %collective-permute-start.1 = (f32[8,64,64]{1,2,0:T(8,128)S(1)}, f32[8,64,64]{1,2,0:T(8,128)S(1)}, u32[]{:S(2)}, u32[]{:S(2)}) collective-permute-start(f32[8,64,64]{1,2,0:T(8,128)S(1)} %copy_multiply_fusion), channel_id=1, source_target_pairs={{0,1},{1,2},{2,3},{3,4},{4,5},{5,6},{6,7},{7,8},{8,9},{9,10},{10,1... | collective-permute-start | bytes 393224 | tf_op jit(solution)/shard_map/ppermute | solution.py:12
  16.7 8.7 %collective-permute-start = (f32[8,64,64]{1,2,0:T(8,128)S(1)}, f32[8,64,64]{1,2,0:T(8,128)S(1)}, u32[]{:S(2)}, u32[]{:S(2)}) collective-permute-start(f32[8,64,64]{1,2,0:T(8,128)S(1)} %copy_multiply_fusion), channel_id=1, source_target_pairs={{0,2},{1,3},{2,4},{3,5},{4,6},{5,7},{6,8},{7,9},{8,10},{9,11},{10,... | collective-permute-start | bytes 393224 | tf_op jit(solution)/shard_map/ppermute | solution.py:12
  58.3 10.2 %collective-permute-start.4 = (f32[8,64,64]{1,2,0:T(8,128)S(1)}, f32[8,64,64]{1,2,0:T(8,128)S(1)}, u32[]{:S(2)}, u32[]{:S(2)}) collective-permute-start(f32[8,64,64]{1,2,0:T(8,128)S(1)} %fusion.4), channel_id=1, source_target_pairs={{0,2},{1,3},{2,4},{3,5},{4,6},{5,7},{6,8},{7,9},{8,10},{9,11},{10,... | collective-permute-start | bytes 393224 | tf_op jit(solution)/shard_map/ppermute | solution.py:12
  62.4 8.9 %collective-permute-start.5 = (f32[8,64,64]{1,2,0:T(8,128)S(1)}, f32[8,64,64]{1,2,0:T(8,128)S(1)}, u32[]{:S(2)}, u32[]{:S(2)}) collective-permute-start(f32[8,64,64]{1,2,0:T(8,128)S(1)} %fusion.4), channel_id=1, source_target_pairs={{0,1},{1,2},{2,3},{3,4},{4,5},{5,6},{6,7},{7,8},{8,9},{9,10},{10,1... | collective-permute-start | bytes 393224 | tf_op jit(solution)/shard_map/ppermute | solution.py:12
  65.1 12.8 %collective-permute-start.7 = (f32[8,64,64]{1,2,0:T(8,128)S(1)}, f32[8,64,64]{1,2,0:T(8,128)S(1)}, u32[]{:S(2)}, u32[]{:S(2)}) collective-permute-start(f32[8,64,64]{1,2,0:T(8,128)S(1)} %fusion.4), channel_id=1, source_target_pairs={{2,0},{3,1},{4,2},{5,3},{6,4},{7,5},{8,6},{9,7},{10,8},{11,9},{12,... | collective-permute-start | bytes 393224 | tf_op jit(solution)/shard_map/ppermute | solution.py:12
  66.4 11.4 %collective-permute-start.6 = (f32[8,64,64]{1,2,0:T(8,128)S(1)}, f32[8,64,64]{1,2,0:T(8,128)S(1)}, u32[]{:S(2)}, u32[]{:S(2)}) collective-permute-start(f32[8,64,64]{1,2,0:T(8,128)S(1)} %fusion.4), channel_id=1, source_target_pairs={{1,0},{2,1},{3,2},{4,3},{5,4},{6,5},{7,6},{8,7},{9,8},{10,9},{11,1... | collective-permute-start | bytes 393224 | tf_op jit(solution)/shard_map/ppermute | solution.py:12
where the time goes:
time: 356 us; the launch traced here: 355 us
  blocking collectives  216 us (61%)
  local copies, waits for them, and re-layouts  43.3 us (12%)
  other arithmetic  32.9 us (9%)
  starting transfers between devices  26.5 us (7%)
  matrix products  21.5 us (6%)
  waiting for transfers between devices  13.8 us (4%)
    psum x2, blocking collectives, summed_gram(): return lax.psum(local_gram, ('grp', 'dev'))  216 us
    ppermute x8, starting transfers between devices, shifted(): return lax.ppermute(block, axis, route)  26.5 us
    dot_general x2, matrix products, apply_matrix(): jnp.einsum('gik,gkc->gic', hamiltonian, picked, precision=lax.Precision.H...  17.4 us
    select_n x2, local copies, waits for them, and re-layouts, apply_matrix(): picked = jnp.take(extended, local_index, axis=0)  16 us
    reshape x2, local copies, waits for them, and re-layouts, apply_matrix(): picked.reshape(block_count, neighbours * values.shape[1], values.shape[2])  15.6 us
    ppermute x8, waiting for transfers between devices, shifted(): return lax.ppermute(block, axis, route)  13.8 us
    another operation x6, other arithmetic, cholesky_step(): upper = jnp.linalg.cholesky(gram_total).T  13.1 us
    another operation x4, other arithmetic, cholesky_step(): ortho = jax.scipy.linalg.solve_triangular(upper.T, flat.T, lower=True).T  11.1 us
  transfers between devices with their start and end apart: 8, of which 3 were waited for; matrix products, arithmetic and copies ran while one was open for 1% of the time, Pallas kernels for 0%

commit v1 on v0

--- a/solution.py
+++ b/solution.py
@@ -38,7 +38,7 @@
     local_gram = jnp.dot(
         flat.T, flat, precision=lax.Precision.HIGHEST, preferred_element_type=jnp.float32
     )
-    return lax.psum(local_gram, ("grp", "dev"))
+    return lax.psum(lax.psum(local_gram, "dev"), "grp")
 
 
 def cholesky_step(flat):

time: 356 us -> 471 us (1.32)
  the two profiles are of different devices: /device:TPU:1 before, /device:TPU:8 now
where the time goes in v1:
time: 471 us; the launch traced here: 470 us
  blocking collectives  326 us (69%)
  local copies, waits for them, and re-layouts  43.3 us (9%)
  other arithmetic  32.9 us (7%)
  starting transfers between devices  31.6 us (7%)
  matrix products  21.5 us (5%)
  waiting for transfers between devices  13.5 us (3%)
    psum x4, blocking collectives, summed_gram(): return lax.psum(lax.psum(local_gram, 'dev'), 'grp')  326 us
    ppermute x8, starting transfers between devices, shifted(): return lax.ppermute(block, axis, route)  31.6 us
    dot_general x2, matrix products, apply_matrix(): jnp.einsum('gik,gkc->gic', hamiltonian, picked, precision=lax.Precision.H...  17.4 us
    select_n x2, local copies, waits for them, and re-layouts, apply_matrix(): picked = jnp.take(extended, local_index, axis=0)  16 us
    reshape x2, local copies, waits for them, and re-layouts, apply_matrix(): picked.reshape(block_count, neighbours * values.shape[1], values.shape[2])  15.6 us
    ppermute x8, waiting for transfers between devices, shifted(): return lax.ppermute(block, axis, route)  13.5 us
    another operation x6, other arithmetic, cholesky_step(): upper = jnp.linalg.cholesky(gram_total).T  13.1 us
    another operation x4, other arithmetic, cholesky_step(): ortho = jax.scipy.linalg.solve_triangular(upper.T, flat.T, lower=True).T  11.1 us
  transfers between devices with their start and end apart: 8, of which 3 were waited for; matrix products, arithmetic and copies ran while one was open for 0% of the time, Pallas kernels for 0%

profile of v1, /device:TPU:8, one launch (start us, length us, event | category | flops | bytes accessed | tf_op | source)
XLA Modules:
  0.0 470.2 jit_solution(5157332896381841652)
XLA Ops:
  2.4 11.3 %collective-permute-start.3 = (f32[8,64,64]{1,2,0:T(8,128)S(1)}, f32[8,64,64]{1,2,0:T(8,128)S(1)}, u32[]{:S(2)}, u32[]{:S(2)}) collective-permute-start(f32[8,64,64]{1,2,0:T(8,128)S(1)} %copy_multiply_fusion), channel_id=1, source_target_pairs={{2,0},{3,1},{4,2},{5,3},{6,4},{7,5},{8,6},{9,7},{10,8},{11,9},{12,... | collective-permute-start | bytes 393224 | tf_op jit(solution)/shard_map/ppermute | solution.py:12
  18.0 2.6 collective-permute-start
  22.7 8.5 %collective-permute-done = f32[8,64,64]{1,2,0:T(8,128)S(1)} collective-permute-done((f32[8,64,64]{1,2,0:T(8,128)S(1)}, f32[8,64,64]{1,2,0:T(8,128)S(1)}, u32[]{:S(2)}, u32[]{:S(2)}) %collective-permute-start) | collective-permute-done | bytes 131104 | tf_op jit(solution)/shard_map/ppermute | solution.py:12
  31.4 4.4 gather_fusion
  35.8 3.8 broadcast_select_fusion.1
  39.6 8.0 %copy.15 = f32[8,32,64,64]{2,1,3,0:T(8,128)} copy(f32[8,32,64,64]{2,3,1,0:T(8,128)S(1)} %broadcast_select_fusion.1) | data formatting | bytes 8388608 | tf_op jit(solution)/shard_map/jit(_take)/select_n | solution.py:32
  47.6 7.8 %reshape.35 = f32[8,2048,64]{1,2,0:T(8,128)} reshape(f32[8,32,64,64]{2,1,3,0:T(8,128)} %copy.15) | data formatting | bytes 8388608 | tf_op jit(solution)/shard_map/reshape | solution.py:33
  55.4 8.7 %fusion.4 = f32[8,64,64]{1,2,0:T(8,128)S(1)} fusion(f32[8,2048,64]{1,2,0:T(8,128)} %reshape.35, f32[8,64,2048]{2,1,0:T(8,128)} %param.11, f32[]{:T(128)} %bitcast.4, f32[]{:T(128)} %bitcast.3, f32[8]{0:T(128)S(1)} %compare_convert_fusion, f32[8,64,64]{1,0,2:T(8,128)S(1)} %reshape.34), kind=kOutput, calls=%fused_computation.10 | convolution fusion | flops 805470208 | bytes 8650792 | tf_op jit(solution)/shard_map/gik,gkc->gic/dot_general | solution.py:34
  68.0 6.0 %collective-permute-start.7 = (f32[8,64,64]{1,2,0:T(8,128)S(1)}, f32[8,64,64]{1,2,0:T(8,128)S(1)}, u32[]{:S(2)}, u32[]{:S(2)}) collective-permute-start(f32[8,64,64]{1,2,0:T(8,128)S(1)} %fusion.4), channel_id=1, source_target_pairs={{2,0},{3,1},{4,2},{5,3},{6,4},{7,5},{8,6},{9,7},{10,8},{11,9},{12,... | collective-permute-start | bytes 393224 | tf_op jit(solution)/shard_map/ppermute | solution.py:12
  74.0 3.5 collective-permute-start.6
  79.2 3.4 collective-permute-done.6
  82.7 4.4 gather_fusion.1
  87.1 3.8 broadcast_select_fusion
  90.9 8.0 %copy.16 = f32[8,32,64,64]{2,1,3,0:T(8,128)} copy(f32[8,32,64,64]{2,3,1,0:T(8,128)S(1)} %broadcast_select_fusion) | data formatting | bytes 8388608 | tf_op jit(solution)/shard_map/jit(_take)/select_n | solution.py:32
  98.9 7.8 %reshape.36 = f32[8,2048,64]{1,2,0:T(8,128)} reshape(f32[8,32,64,64]{2,1,3,0:T(8,128)} %copy.16) | data formatting | bytes 8388608 | tf_op jit(solution)/shard_map/reshape | solution.py:33
  106.7 8.7 %fusion.7 = f32[8,64,64]{1,2,0:T(8,128)S(1)} fusion(f32[8,2048,64]{1,2,0:T(8,128)} %reshape.36, f32[8,64,2048]{2,1,0:T(8,128)} %param.11, f32[8,64,64]{1,2,0:T(8,128)S(1)} %fusion.4, f32[]{:T(128)} %bitcast.4, f32[]{:T(128)} %bitcast.3, f32[8]{0:T(128)S(1)} %compare_convert_fusion, f32[8,64,64]{1,0,2:T(8,128)S(1)} %reshape.34), kind=kOutput, calls=%fused_computation.13 | convolution fusion | flops 805535744 | bytes 8781864 | tf_op jit(solution)/shard_map/gik,gkc->gic/dot_general | solution.py:34
  116.1 94.1 %psum.28 = f32[64,64]{0,1:T(8,128)S(1)} all-reduce(f32[64,64]{0,1:T(8,128)S(1)} %convolution_bitcast_fusion.2), channel_id=1, replica_groups=mesh['grp'=16,'dev'=32] {'dev'}, use_global_device_ids=true, to_apply=%region_0.0 | all-reduce | flops 4096 | bytes 32768 | tf_op jit(solution)/shard_map/psum | solution.py:41
  210.2 70.1 %psum.29 = f32[64,64]{0,1:T(8,128)S(1)} all-reduce(f32[64,64]{0,1:T(8,128)S(1)} %psum.28), channel_id=1, replica_groups=mesh['grp'=16,'dev'=32] {'grp'}, use_global_device_ids=true, to_apply=%region_1.3 | all-reduce | flops 4096 | bytes 32768 | tf_op jit(solution)/shard_map/psum | solution.py:41
  280.4 5.8 %cholesky.44 = f32[64,64]{1,0:T(8,128)S(1)} custom-call(f32[64,64]{1,0:T(8,128)S(1)} %fusion.14), custom_call_target="Cholesky" | custom-call | tf_op jit(solution)/shard_map/jit(cholesky)/cholesky | solution.py:46
  287.6 4.9 %custom-call.6 = f32[1,64,64]{1,2,0:T(8,128)S(1)} custom-call(f32[1,64,64]{2,1,0:T(8,128)S(1)} %fusion.18), custom_call_target="InvertDiagBlocksLowerTriangular" | custom-call | tf_op jit(solution)/shard_map/jit(_solve_triangular)/triangular_solve | solution.py:47
  293.1 90.0 %psum.30 = f32[64,64]{0,1:T(8,128)S(1)} all-reduce(f32[64,64]{0,1:T(8,128)S(1)} %fusion.30), channel_id=1, replica_groups=mesh['grp'=16,'dev'=32] {'dev'}, use_global_device_ids=true, to_apply=%region_4.8 | all-reduce | flops 4096 | bytes 32768 | tf_op jit(solution)/shard_map/psum | solution.py:41
  383.1 71.7 %psum.31 = f32[64,64]{0,1:T(8,128)S(1)} all-reduce(f32[64,64]{0,1:T(8,128)S(1)} %psum.30), channel_id=1, replica_groups=mesh['grp'=16,'dev'=32] {'grp'}, use_global_device_ids=true, to_apply=%region_5.9 | all-reduce | flops 4096 | bytes 32768 | tf_op jit(solution)/shard_map/psum | solution.py:41
  454.8 5.8 %cholesky.55 = f32[64,64]{1,0:T(8,128)S(1)} custom-call(f32[64,64]{1,0:T(8,128)S(1)} %fusion.12), custom_call_target="Cholesky" | custom-call | tf_op jit(solution)/shard_map/jit(cholesky)/cholesky | solution.py:46
  464.3 4.9 %custom-call.7 = f32[1,64,64]{1,2,0:T(8,128)S(1)} custom-call(f32[1,64,64]{2,1,0:T(8,128)S(1)} %select_bitcast_fusion), custom_call_target="InvertDiagBlocksLowerTriangular" | custom-call | tf_op jit(solution)/shard_map/jit(_solve_triangular)/triangular_solve | solution.py:47
  (44 shorter events, 20.6 us)
Async XLA Ops:
  2.4 29.0 %collective-permute-start.3 = (f32[8,64,64]{1,2,0:T(8,128)S(1)}, f32[8,64,64]{1,2,0:T(8,128)S(1)}, u32[]{:S(2)}, u32[]{:S(2)}) collective-permute-start(f32[8,64,64]{1,2,0:T(8,128)S(1)} %copy_multiply_fusion), channel_id=1, source_target_pairs={{2,0},{3,1},{4,2},{5,3},{6,4},{7,5},{8,6},{9,7},{10,8},{11,9},{12,... | collective-permute-start | bytes 393224 | tf_op jit(solution)/shard_map/ppermute | solution.py:12
  13.7 17.7 %collective-permute-start.2 = (f32[8,64,64]{1,2,0:T(8,128)S(1)}, f32[8,64,64]{1,2,0:T(8,128)S(1)}, u32[]{:S(2)}, u32[]{:S(2)}) collective-permute-start(f32[8,64,64]{1,2,0:T(8,128)S(1)} %copy_multiply_fusion), channel_id=1, source_target_pairs={{1,0},{2,1},{3,2},{4,3},{5,4},{6,5},{7,6},{8,7},{9,8},{10,9},{11,1... | collective-permute-start | bytes 393224 | tf_op jit(solution)/shard_map/ppermute | solution.py:12
  15.8 15.4 %collective-permute-start.1 = (f32[8,64,64]{1,2,0:T(8,128)S(1)}, f32[8,64,64]{1,2,0:T(8,128)S(1)}, u32[]{:S(2)}, u32[]{:S(2)}) collective-permute-start(f32[8,64,64]{1,2,0:T(8,128)S(1)} %copy_multiply_fusion), channel_id=1, source_target_pairs={{0,1},{1,2},{2,3},{3,4},{4,5},{5,6},{6,7},{7,8},{8,9},{9,10},{10,1... | collective-permute-start | bytes 393224 | tf_op jit(solution)/shard_map/ppermute | solution.py:12
  18.0 13.2 %collective-permute-start = (f32[8,64,64]{1,2,0:T(8,128)S(1)}, f32[8,64,64]{1,2,0:T(8,128)S(1)}, u32[]{:S(2)}, u32[]{:S(2)}) collective-permute-start(f32[8,64,64]{1,2,0:T(8,128)S(1)} %copy_multiply_fusion), channel_id=1, source_target_pairs={{0,2},{1,3},{2,4},{3,5},{4,6},{5,7},{6,8},{7,9},{8,10},{9,11},{10,... | collective-permute-start | bytes 393224 | tf_op jit(solution)/shard_map/ppermute | solution.py:12
  64.1 13.4 %collective-permute-start.4 = (f32[8,64,64]{1,2,0:T(8,128)S(1)}, f32[8,64,64]{1,2,0:T(8,128)S(1)}, u32[]{:S(2)}, u32[]{:S(2)}) collective-permute-start(f32[8,64,64]{1,2,0:T(8,128)S(1)} %fusion.4), channel_id=1, source_target_pairs={{0,2},{1,3},{2,4},{3,5},{4,6},{5,7},{6,8},{7,9},{8,10},{9,11},{10,... | collective-permute-start | bytes 393224 | tf_op jit(solution)/shard_map/ppermute | solution.py:12
  66.1 13.1 %collective-permute-start.5 = (f32[8,64,64]{1,2,0:T(8,128)S(1)}, f32[8,64,64]{1,2,0:T(8,128)S(1)}, u32[]{:S(2)}, u32[]{:S(2)}) collective-permute-start(f32[8,64,64]{1,2,0:T(8,128)S(1)} %fusion.4), channel_id=1, source_target_pairs={{0,1},{1,2},{2,3},{3,4},{4,5},{5,6},{6,7},{7,8},{8,9},{9,10},{10,1... | collective-permute-start | bytes 393224 | tf_op jit(solution)/shard_map/ppermute | solution.py:12
  68.0 14.7 %collective-permute-start.7 = (f32[8,64,64]{1,2,0:T(8,128)S(1)}, f32[8,64,64]{1,2,0:T(8,128)S(1)}, u32[]{:S(2)}, u32[]{:S(2)}) collective-permute-start(f32[8,64,64]{1,2,0:T(8,128)S(1)} %fusion.4), channel_id=1, source_target_pairs={{2,0},{3,1},{4,2},{5,3},{6,4},{7,5},{8,6},{9,7},{10,8},{11,9},{12,... | collective-permute-start | bytes 393224 | tf_op jit(solution)/shard_map/ppermute | solution.py:12
  74.0 8.6 %collective-permute-start.6 = (f32[8,64,64]{1,2,0:T(8,128)S(1)}, f32[8,64,64]{1,2,0:T(8,128)S(1)}, u32[]{:S(2)}, u32[]{:S(2)}) collective-permute-start(f32[8,64,64]{1,2,0:T(8,128)S(1)} %fusion.4), channel_id=1, source_target_pairs={{1,0},{2,1},{3,2},{4,3},{5,4},{6,5},{7,6},{8,7},{9,8},{10,9},{11,1... | collective-permute-start | bytes 393224 | tf_op jit(solution)/shard_map/ppermute | solution.py:12
